TPU v7x, 32 devices: a whole 2x2x4 slice. The times are simulated.
32 devices in a mesh: parts: 2 (over x), lon: 16 (over z, y, core).
Axes of the slice: x: 2, y: 2, z: 4, core: 2. Of those that a mesh axis runs over, the one named last changes fastest.
Arguments:
- solution: float32 [2048, 32, 512], P(('parts', 'lon')), parts along dimension 0, may hold values from -6 to 6
- residual: float32 [2048, 32, 512], P(('parts', 'lon')), parts along dimension 0, may hold values from -12 to 12
- direction: float32 [2048, 32, 512], P(('parts', 'lon')), parts along dimension 0, may hold values from -12 to 12
- land: int32 [2048, 512], P(('parts', 'lon')), parts along dimension 0, may hold values 0 or 1
- clear: int32 [2048, 32, 512], P(('parts', 'lon')), parts along dimension 0, may hold values 0 or 1
- days: int32 [64], P('parts'), parts along dimension 0, may hold values from 0 to 63, as said below
- mixture: float32 [6, 3, 4], P('parts'), parts along dimension 0, may hold values from 0 to 1024, as said below
- q_lon: bfloat16 [1024, 1024], replicated, may hold values from -0.1875 to 0.1875
- q_lat: bfloat16 [512, 512], replicated, may hold values from -0.25 to 0.25
- q_day: bfloat16 [64, 32], P('parts'), parts along dimension 0, may hold values from -1 to 1
- lam_lon: float32 [1024], replicated, may hold values from 0.2 to 5
- lam_lat: float32 [512], replicated, may hold values from 0.2 to 5
- lam_day: float32 [64], P('parts'), parts along dimension 0, may hold values from 0.2 to 5
- noise: float32 [2], P('parts'), parts along dimension 0, may hold values from 0.5 to 2
- rz_mean: float32 [2], P('parts'), parts along dimension 0, may hold values from 0.25 to 1
Outputs:
- new_solution: float32 [2048, 32, 512], P(('parts', 'lon')), parts along dimension 0
- new_residual: float32 [2048, 32, 512], P(('parts', 'lon')), parts along dimension 0
- new_direction: float32 [2048, 32, 512], P(('parts', 'lon')), parts along dimension 0
- new_rz_mean: float32 [2], P('parts'), parts along dimension 0
There are 2 independent parts, one for each index of `parts`. A program takes and returns all parts, laid end to end along the dimension named above; an argument that names none is the same for every part. Nothing has to cross between parts.
Inputs may be any that keep to these rules, and one draw needn't show every extreme that they name: days[k] is 2 k or 2 k + 1, so the days rise strictly within a record of 64 days; the first is 0 and the last 63. mixture[g, 0] are positive weights, mixture[g, 1] frequencies of at most one half per cell or day, mixture[g, 2] positive length scales in cells or days.
All inputs are finite; a program needn't handle non-finite values. No bound on the sum of `land` or of `clear` on one device may be relied on, other than what follows from the above.
Results may differ from a plain program's by a relative error of at most 0.0018.
Values may be sent and summed in bfloat16 or wider, within the bound.
A program may use at most 128 MiB of HBM per device.

v0:
```python
import math
import jax
import jax.numpy as jnp
from jax import lax
from jax.sharding import PartitionSpec as P


def kernel_factor(left, right, params):
    diff = left[:, None] - right[None, :]
    total = jnp.zeros(diff.shape, jnp.float32)
    for comp in range(params.shape[1]):
        weight = params[0, comp]
        freq = params[1, comp]
        length = params[2, comp]
        ratio = diff / length
        total = total + weight * jnp.exp(-0.5 * ratio * ratio) * jnp.cos(
            2.0 * math.pi * freq * diff
        )
    return total.astype(jnp.bfloat16)


def to_exchanged(block):
    flat = block.reshape(block.shape[0], -1)
    return lax.all_to_all(flat, "lon", split_axis=1, concat_axis=0, tiled=True)


def to_longitude(wide, shape):
    back = lax.all_to_all(wide, "lon", split_axis=0, concat_axis=1, tiled=True)
    return back.reshape(shape)


def day_product(matrix, field):
    return jnp.einsum("ck,akb->acb", matrix, field, preferred_element_type=jnp.float32)


def day_product_transposed(matrix, field):
    return jnp.einsum("kc,akb->acb", matrix, field, preferred_element_type=jnp.float32)


def lat_product(matrix, field):
    return jnp.einsum("acj,bj->acb", field, matrix, preferred_element_type=jnp.float32)


def lat_product_transposed(matrix, field):
    return jnp.einsum("acj,jb->acb", field, matrix, preferred_element_type=jnp.float32)


def lon_product_transposed(matrix, wide):
    return lax.dot_general(
        matrix, wide, (((0,), (0,)), ((), ())), preferred_element_type=jnp.float32
    )


def on_device(
    solution,
    residual,
    direction,
    land,
    clear,
    days,
    mixture,
    q_lon,
    q_lat,
    q_day,
    lam_lon,
    lam_lat,
    lam_day,
    noise,
    rz_mean,
):
    bf = jnp.bfloat16
    shape = solution.shape
    lon_dev, n_days, n_lat = shape
    n_lon = q_lon.shape[0]
    cells = n_lon * n_days * n_lat
    observed = (land[:, None, :] * clear).astype(jnp.float32)
    sigma = noise[0]
    lon_pos = jnp.arange(n_lon, dtype=jnp.float32)
    lat_pos = jnp.arange(n_lat, dtype=jnp.float32)
    day_pos = days.astype(jnp.float32)
    k_lon = kernel_factor(lon_pos, lon_pos, mixture[0])
    k_lat = kernel_factor(lat_pos, lat_pos, mixture[1])
    k_day = kernel_factor(day_pos, day_pos, mixture[2])
    first = (observed * direction).astype(bf)
    second = day_product(k_day, first).astype(bf)
    third = lat_product(k_lat, second).astype(bf)
    spread = to_exchanged(third)
    fourth = jnp.dot(k_lon, spread, preferred_element_type=jnp.float32).astype(bf)
    returned = to_longitude(fourth, shape)
    image = observed * (returned.astype(jnp.float32) + sigma * direction)
    curvature = lax.psum(jnp.sum(direction * image), "lon")
    alpha = rz_mean[0] * cells / curvature
    new_solution = solution + alpha * direction
    new_residual = residual - alpha * image
    g_zero = (observed * new_residual).astype(bf)
    g_one = day_product_transposed(q_day, g_zero).astype(bf)
    g_two = lat_product_transposed(q_lat, g_one).astype(bf)
    spread_g = to_exchanged(g_two)
    g_three = lon_product_transposed(q_lon, spread_g).astype(bf)
    g_local = to_longitude(g_three, shape)
    lon_rows = lax.dynamic_slice_in_dim(lam_lon, lax.axis_index("lon") * lon_dev, lon_dev)
    denom = lon_rows[:, None, None] * lam_day[None, :, None] * lam_lat[None, None, :] + sigma
    scaled = (g_local.astype(jnp.float32) / denom).astype(bf)
    spread_h = to_exchanged(scaled)
    h_one = jnp.dot(q_lon, spread_h, preferred_element_type=jnp.float32).astype(bf)
    h_local = to_longitude(h_one, shape)
    h_two = lat_product(q_lat, h_local).astype(bf)
    precond = observed * day_product(q_day, h_two)
    total = lax.psum(jnp.sum(new_residual * precond), "lon")
    new_rz = total / cells
    new_direction = precond + new_rz / rz_mean[0] * direction
    return (new_solution, new_residual, new_direction, new_rz.reshape(1))


def solution(mesh):
    in_specs = (
        P(("parts", "lon"), None, None),
        P(("parts", "lon"), None, None),
        P(("parts", "lon"), None, None),
        P(("parts", "lon"), None),
        P(("parts", "lon"), None, None),
        P("parts"),
        P("parts", None, None),
        P(),
        P(),
        P("parts", None),
        P(),
        P(),
        P("parts"),
        P("parts"),
        P("parts"),
    )
    out_specs = (
        P(("parts", "lon"), None, None),
        P(("parts", "lon"), None, None),
        P(("parts", "lon"), None, None),
        P("parts"),
    )
    return jax.shard_map(
        on_device, mesh=mesh, in_specs=in_specs, out_specs=out_specs, check_vma=False
    )
```

profile of v0, /device:TPU:0, one launch (start us, length us, event | category | flops | bytes accessed | tf_op | source)
XLA Modules:
  0.0 581.4 jit_solution(6673061924529932363)
XLA Ops:
  8.6 31.5 %fusion.50 = bf16[64,32,512]{2,1,0:T(8,128)(2,1)} fusion(f32[64,32,512]{2,1,0:T(8,128)} %param.17, s32[64,32,512]{2,1,0:T(8,128)} %param.19, s32[64,512]{1,0:T(8,128)} %param.18, f32[]{:T(128)} %bitcast.41, f32[]{:T(128)} %bitcast.40, f32[]{:T(128)} %bitcast.39, f32[]{:T(128)} %bitcast.38, f32[]{:T(128)} %bitcast.37, f32[]{:T(128)} %bitcast.36, ...), kind=kOutput, calls=%fused_computation.59 | convolution fusion | flops 1154774016 | bytes 10617056 | tf_op jit(solution)/shard_map/acj,bj->acb/dot_general | solution.py:41
  40.1 4.1 all_to_all.72
  44.1 4.1 copy.32
  48.2 7.4 %all-to-all-start = ((bf16[64,16,1024]{2,0,1:T(8,128)(2,1)}), bf16[64,16,1024]{2,0,1:T(8,128)(2,1)}, u32[]{:S(2)}, u32[]{:S(2)}) async-start(bf16[64,16,1024]{2,0,1:T(8,128)(2,1)} %copy.32), calls=%async_computation | async-start | bytes 4194304 | tf_op jit(solution)/shard_map/all_to_all | solution.py:24
  58.8 38.0 %all-to-all-done = bf16[64,16,1024]{2,0,1:T(8,128)(2,1)} async-done(((bf16[64,16,1024]{2,0,1:T(8,128)(2,1)}), bf16[64,16,1024]{2,0,1:T(8,128)(2,1)}, u32[]{:S(2)}, u32[]{:S(2)}) %all-to-all-start) | async-done | bytes 2097184 | tf_op jit(solution)/shard_map/all_to_all | solution.py:24
  96.8 67.8 %fusion.47 = bf16[1024,1024]{1,0:T(8,128)(2,1)} fusion(bf16[1024,1024]{1,0:T(8,128)(2,1)} %bitcast.44, f32[]{:T(128)} %bitcast.13, f32[]{:T(128)} %bitcast.12, f32[]{:T(128)} %bitcast.11, f32[]{:T(128)} %bitcast.10, f32[]{:T(128)} %bitcast.9, f32[]{:T(128)} %bitcast.8, f32[]{:T(128)} %bitcast.7, f32[]{:T(128)} %bitcast.6, f32[]{:T(128)} %bitcast.5, ...), kind=kOutput, calls=%fused_computation.58 | convolution fusion | flops 2178940928 | bytes 4194352 | tf_op jit(solution)/shard_map/dot_general | solution.py:88
  164.6 11.3 %all-to-all-start.1 = ((bf16[16,64,1024]{2,1,0:T(8,128)(2,1)}), bf16[16,64,1024]{2,1,0:T(8,128)(2,1)}, u32[]{:S(2)}, u32[]{:S(2)}) async-start(bf16[16,64,1024]{2,1,0:T(8,128)(2,1)} %bitcast.121), calls=%async_computation.1 | async-start | bytes 4194304 | tf_op jit(solution)/shard_map/all_to_all | solution.py:28
  177.2 39.9 %all-to-all-done.1 = bf16[16,64,1024]{2,1,0:T(8,128)(2,1)} async-done(((bf16[16,64,1024]{2,1,0:T(8,128)(2,1)}), bf16[16,64,1024]{2,1,0:T(8,128)(2,1)}, u32[]{:S(2)}, u32[]{:S(2)}) %all-to-all-start.1) | async-done | bytes 2097184 | tf_op jit(solution)/shard_map/all_to_all | solution.py:28
  217.1 2.0 convert_bitcast_fusion
  219.1 4.4 copy.33
  223.6 5.0 reshape.116
  228.5 6.9 %multiply_reduce_fusion.1 = f32[]{:T(128)} fusion(f32[64,32,512]{2,1,0:T(8,128)} %param.17, f32[64,32,512]{2,1,0:T(8,128)} %reshape.116, f32[]{:T(128)} %bitcast.114, s32[64,32,512]{2,1,0:T(8,128)} %param.19, s32[64,512]{1,0:T(8,128)S(1)} %copy-done.1), kind=kLoop, calls=%fused_computation.29 | loop fusion | flops 7340031 | bytes 12713992 | tf_op jit(solution)/shard_map/reduce_sum | solution.py:91
  235.4 39.8 %psum.14 = f32[]{:T(128)} all-reduce(f32[]{:T(128)} %multiply_reduce_fusion.1), channel_id=1, replica_groups=mesh['parts'=2,'lon'=16] {'lon'}, use_global_device_ids=true, to_apply=%region_1.0 | all-reduce | flops 1 | bytes 8 | tf_op jit(solution)/shard_map/psum | solution.py:91
  275.9 10.5 %multiply_subtract_fusion = f32[64,32,512]{2,1,0:T(8,128)} fusion(f32[64,32,512]{2,1,0:T(8,128)} %param.16, f32[]{:T(128)S(6)} %div.110, f32[64,32,512]{2,1,0:T(8,128)} %reshape.116, f32[64,32,512]{2,1,0:T(8,128)} %param.17, f32[]{:T(128)} %bitcast.116, s32[64,32,512]{2,1,0:T(8,128)} %param.19, s32[64,512]{1,0:T(8,128)S(1)} %copy-done.1), kind=kLoop, calls=%fused_computation.27 | loop fusion | flops 7340032 | bytes 21102600 | tf_op jit(solution)/shard_map/sub | solution.py:94
  286.4 7.3 %fusion.53 = bf16[64,32,512]{2,1,0:T(8,128)(2,1)} fusion(f32[64,32,512]{2,1,0:T(8,128)} %multiply_subtract_fusion, s32[64,32,512]{2,1,0:T(8,128)} %param.19, s32[64,512]{1,0:T(8,128)S(1)} %copy-done.1, bf16[512,512]{1,0:T(8,128)(2,1)S(1)} %copy-done.2, bf16[32,32]{1,0:T(8,128)(2,1)S(1)} %copy-done.3), kind=kOutput, calls=%fused_computation.60 | convolution fusion | flops 1147142144 | bytes 11143168 | tf_op jit(solution)/shard_map/acj,jb->acb/dot_general | solution.py:45
  293.7 4.1 all_to_all.78
  297.8 2.7 copy.35
  300.5 50.1 %all_to_all.96 = bf16[64,16,1024]{2,0,1:T(8,128)(2,1)S(1)} all-to-all(bf16[64,16,1024]{2,0,1:T(8,128)(2,1)S(1)} %copy.35), channel_id=1, replica_groups=mesh['parts'=2,'lon'=16] {'lon'}, dimensions={1} | all-to-all | bytes 4194304 | tf_op jit(solution)/shard_map/all_to_all | solution.py:24
  350.6 3.7 convolution_convert_fusion.1
  354.4 5.1 all-to-all-start.3
  360.4 2.4 mul.543
  362.7 5.2 mul.544
  367.9 32.7 %all-to-all-done.3 = bf16[16,64,1024]{2,1,0:T(8,128)(2,1)} async-done(((bf16[16,64,1024]{2,1,0:T(8,128)(2,1)}), bf16[16,64,1024]{2,1,0:T(8,128)(2,1)}, u32[]{:S(2)}, u32[]{:S(2)}) %all-to-all-start.3) | async-done | bytes 2097184 | tf_op jit(solution)/shard_map/all_to_all | solution.py:28
  400.7 4.3 fusion.16
  406.2 58.3 %all_to_all.97 = bf16[64,16,1024]{2,0,1:T(8,128)(2,1)S(1)} all-to-all(bf16[64,16,1024]{2,0,1:T(8,128)(2,1)S(1)} %copy.37), channel_id=1, replica_groups=mesh['parts'=2,'lon'=16] {'lon'}, dimensions={1} | all-to-all | bytes 4194304 | tf_op jit(solution)/shard_map/all_to_all | solution.py:24
  464.5 2.4 convolution_convert_fusion
  466.9 52.5 %all_to_all.98 = bf16[16,64,1024]{2,1,0:T(8,128)(2,1)S(1)} all-to-all(bf16[16,64,1024]{2,1,0:T(8,128)(2,1)S(1)} %bitcast.124), channel_id=1, replica_groups=mesh['parts'=2,'lon'=16] {'lon'}, dimensions={0} | all-to-all | bytes 4194304 | tf_op jit(solution)/shard_map/all_to_all | solution.py:28
  519.3 2.5 copy.38
  521.8 4.1 reshape.114
  525.9 9.0 %multiply_reduce_fusion = (f32[]{:T(128)}, f32[64,32,512]{2,1,0:T(8,128)}) fusion(f32[64,32,512]{2,1,0:T(8,128)} %multiply_subtract_fusion, bf16[64,32,512]{2,1,0:T(8,128)(2,1)} %reshape.114, bf16[512,512]{1,0:T(8,128)(2,1)S(1)} %copy-done.2, bf16[32,32]{1,0:T(8,128)(2,1)S(1)} %copy-done.3, s32[64,32,512]{2,1,0:T(8,128)} %param.19, s32[64,512]{1,0:T(8,128)S(1)} %copy-done.1), kind=kOutput, calls=%fused_computation.25 | convolution fusion | flops 1147142144 | bytes 15337476 | tf_op jit(solution)/shard_map/ck,akb->acb/dot_general | solution.py:33
  534.9 33.7 %psum.15 = f32[]{:T(128)} all-reduce(f32[]{:T(128)} %get-tuple-element.45), channel_id=1, replica_groups=mesh['parts'=2,'lon'=16] {'lon'}, use_global_device_ids=true, to_apply=%region_3.0 | all-reduce | flops 1 | bytes 8 | tf_op jit(solution)/shard_map/psum | solution.py:109
  569.3 10.6 %multiply_add_fusion = (f32[64,32,512]{2,1,0:T(8,128)}, f32[64,32,512]{2,1,0:T(8,128)}) fusion(f32[64,32,512]{2,1,0:T(8,128)} %get-tuple-element.46, f32[64,32,512]{2,1,0:T(8,128)} %param.17, f32[]{:T(128)S(6)} %div.113, f32[64,32,512]{2,1,0:T(8,128)} %param.15, f32[]{:T(128)S(6)} %div.110), kind=kLoop, calls=%fused_computation.24 | loop fusion | flops 4194304 | bytes 20971528 | tf_op jit(solution)/shard_map/add | solution.py:111
  (22 shorter events, 5.6 us)
Async XLA Ops:
  0.6 350.0 %copy-start = (bf16[1024,1024]{1,0:T(8,128)(2,1)S(1)}, bf16[1024,1024]{1,0:T(8,128)(2,1)}, u32[]{:S(2)}) copy-start(bf16[1024,1024]{1,0:T(8,128)(2,1)} %param.22) | copy-start | bytes 6291460
  48.2 48.6 %all-to-all-start = ((bf16[64,16,1024]{2,0,1:T(8,128)(2,1)}), bf16[64,16,1024]{2,0,1:T(8,128)(2,1)}, u32[]{:S(2)}, u32[]{:S(2)}) async-start(bf16[64,16,1024]{2,0,1:T(8,128)(2,1)} %copy.32), calls=%async_computation | async-start | bytes 4194304 | tf_op jit(solution)/shard_map/all_to_all | solution.py:24
  164.6 52.4 %all-to-all-start.1 = ((bf16[16,64,1024]{2,1,0:T(8,128)(2,1)}), bf16[16,64,1024]{2,1,0:T(8,128)(2,1)}, u32[]{:S(2)}, u32[]{:S(2)}) async-start(bf16[16,64,1024]{2,1,0:T(8,128)(2,1)} %bitcast.121), calls=%async_computation.1 | async-start | bytes 4194304 | tf_op jit(solution)/shard_map/all_to_all | solution.py:28
  223.6 5.0 copy-start.1
  275.9 10.6 %copy-start.2 = (bf16[512,512]{1,0:T(8,128)(2,1)S(1)}, bf16[512,512]{1,0:T(8,128)(2,1)}, u32[]{:S(2)}) copy-start(bf16[512,512]{1,0:T(8,128)(2,1)} %param.23) | copy-start | bytes 1572868
  275.9 10.5 %copy-start.3 = (bf16[32,32]{1,0:T(8,128)(2,1)S(1)}, bf16[32,32]{1,0:T(8,128)(2,1)}, u32[]{:S(2)}) copy-start(bf16[32,32]{1,0:T(8,128)(2,1)} %param.24) | copy-start | bytes 6148
  354.4 5.1 copy-start.4
  354.4 5.9 %copy-start.5 = (f32[32]{0:T(128)S(1)}, f32[32]{0:T(128)}, u32[]{:S(2)}) copy-start(f32[32]{0:T(128)} %param.27) | copy-start | bytes 388
  354.4 46.3 %all-to-all-start.3 = ((bf16[16,64,1024]{2,1,0:T(8,128)(2,1)}), bf16[16,64,1024]{2,1,0:T(8,128)(2,1)}, u32[]{:S(2)}, u32[]{:S(2)}) async-start(bf16[16,64,1024]{2,1,0:T(8,128)(2,1)} %bitcast.120), calls=%async_computation.3 | async-start | bytes 4194304 | tf_op jit(solution)/shard_map/all_to_all | solution.py:28
where the time goes:
time: 591 us; the launch traced here: 581 us
  blocking collectives  234 us (40%)
  matrix products  122 us (21%)
  waiting for transfers between devices  111 us (19%)
  local copies, waits for them, and re-layouts  43.2 us (7%)
  other arithmetic  35.3 us (6%)
  starting transfers between devices  23.8 us (4%)
  between operations  12.5 us (2%)
    all_to_all x2, blocking collectives, to_exchanged(): return lax.all_to_all(flat, 'lon', split_axis=1, concat_axis=0, tiled=True)  108 us
    all_to_all x2, waiting for transfers between devices, to_longitude(): back = lax.all_to_all(wide, 'lon', split_axis=0, concat_axis=1, tiled=True)  72.6 us
    dot_general x1, matrix products, on_device(): jnp.dot(k_lon, spread, preferred_element_type=jnp.float32).astype(bf)  67.8 us
    all_to_all x1, blocking collectives, to_longitude(): back = lax.all_to_all(wide, 'lon', split_axis=0, concat_axis=1, tiled=True)  52.5 us
    psum x1, blocking collectives, on_device(): curvature = lax.psum(jnp.sum(direction * image), 'lon')  39.8 us
    all_to_all x1, waiting for transfers between devices, to_exchanged(): return lax.all_to_all(flat, 'lon', split_axis=1, concat_axis=0, tiled=True)  38 us
    psum x1, blocking collectives, on_device(): total = lax.psum(jnp.sum(new_residual * precond), 'lon')  33.7 us
    dot_general x1, matrix products, lat_product(): jnp.einsum('acj,bj->acb', field, matrix, preferred_element_type=jnp.float32)  31.5 us
  transfers between devices with their start and end apart: 3, of which 3 were waited for; matrix products, arithmetic and copies ran while one was open for 2% of the time, Pallas kernels for 0%

commit v1 on v0

--- a/solution.py
+++ b/solution.py
@@ -25,7 +25,10 @@
 
 
 def to_longitude(wide, shape):
-    back = lax.all_to_all(wide, "lon", split_axis=0, concat_axis=1, tiled=True)
+    back = jnp.concatenate(
+        lax.all_to_all(jnp.stack(jnp.split(wide, lax.axis_size("lon"), axis=0)), "lon", 0, 0),
+        axis=1,
+    )
     return back.reshape(shape)
 
 

time: 591 us -> 611 us (1.034)
  local copies, waits for them, and re-layouts: 43.2 us -> 63.4 us
    unnamed x14 -> x59, local copies, waits for them, and re-layouts: 0.04 us -> 20.1 us
where the time goes in v1:
time: 611 us; the launch traced here: 601 us
  blocking collectives  234 us (38%)
  matrix products  120 us (20%)
  waiting for transfers between devices  111 us (18%)
  local copies, waits for them, and re-layouts  63.4 us (10%)
  other arithmetic  36.3 us (6%)
  starting transfers between devices  23.8 us (4%)
  between operations  12.6 us (2%)
    all_to_all x2, blocking collectives, to_exchanged(): return lax.all_to_all(flat, 'lon', split_axis=1, concat_axis=0, tiled=True)  108 us
    all_to_all x2, waiting for transfers between devices, to_longitude(): lax.all_to_all(jnp.stack(jnp.split(wide, lax.axis_size('lon'), axis=0)),...  72.6 us
    dot_general x1, matrix products, on_device(): jnp.dot(k_lon, spread, preferred_element_type=jnp.float32).astype(bf)  67 us
    all_to_all x1, blocking collectives, to_longitude(): lax.all_to_all(jnp.stack(jnp.split(wide, lax.axis_size('lon'), axis=0)),...  52.5 us
    psum x1, blocking collectives, on_device(): curvature = lax.psum(jnp.sum(direction * image), 'lon')  39.8 us
    all_to_all x1, waiting for transfers between devices, to_exchanged(): return lax.all_to_all(flat, 'lon', split_axis=1, concat_axis=0, tiled=True)  38 us
    psum x1, blocking collectives, on_device(): total = lax.psum(jnp.sum(new_residual * precond), 'lon')  33.7 us
    dot_general x1, matrix products, lat_product(): jnp.einsum('acj,bj->acb', field, matrix, preferred_element_type=jnp.float32)  31.5 us
  transfers between devices with their start and end apart: 3, of which 3 were waited for; matrix products, arithmetic and copies ran while one was open for 2% of the time, Pallas kernels for 0%

profile of v1, /device:TPU:0, one launch (start us, length us, event | category | flops | bytes accessed | tf_op | source)
XLA Modules:
  0.0 600.7 jit_solution(3457881618662303230)
XLA Ops:
  8.6 31.5 %fusion.51 = bf16[64,32,512]{2,1,0:T(8,128)(2,1)} fusion(f32[64,32,512]{2,1,0:T(8,128)} %param.17, s32[64,32,512]{2,1,0:T(8,128)} %param.19, s32[64,512]{1,0:T(8,128)} %param.18, f32[]{:T(128)} %bitcast.41, f32[]{:T(128)} %bitcast.40, f32[]{:T(128)} %bitcast.39, f32[]{:T(128)} %bitcast.38, f32[]{:T(128)} %bitcast.37, f32[]{:T(128)} %bitcast.36, ...), kind=kOutput, calls=%fused_computation.63 | convolution fusion | flops 1154774016 | bytes 10617056 | tf_op jit(solution)/shard_map/acj,bj->acb/dot_general | solution.py:44
  40.1 4.1 all_to_all.49
  44.1 4.1 copy.19
  48.2 7.4 %all-to-all-start = ((bf16[64,16,1024]{2,0,1:T(8,128)(2,1)}), bf16[64,16,1024]{2,0,1:T(8,128)(2,1)}, u32[]{:S(2)}, u32[]{:S(2)}) async-start(bf16[64,16,1024]{2,0,1:T(8,128)(2,1)} %copy.19), calls=%async_computation | async-start | bytes 4194304 | tf_op jit(solution)/shard_map/all_to_all | solution.py:24
  58.8 38.0 %all-to-all-done = bf16[64,16,1024]{2,0,1:T(8,128)(2,1)} async-done(((bf16[64,16,1024]{2,0,1:T(8,128)(2,1)}), bf16[64,16,1024]{2,0,1:T(8,128)(2,1)}, u32[]{:S(2)}, u32[]{:S(2)}) %all-to-all-start) | async-done | bytes 2097184 | tf_op jit(solution)/shard_map/all_to_all | solution.py:24
  96.8 67.0 %fusion.48 = bf16[1024,1024]{1,0:T(8,128)(2,1)S(1)} fusion(bf16[1024,1024]{1,0:T(8,128)(2,1)} %bitcast.44, f32[]{:T(128)} %bitcast.13, f32[]{:T(128)} %bitcast.12, f32[]{:T(128)} %bitcast.11, f32[]{:T(128)} %bitcast.10, f32[]{:T(128)} %bitcast.9, f32[]{:T(128)} %bitcast.8, f32[]{:T(128)} %bitcast.7, f32[]{:T(128)} %bitcast.6, f32[]{:T(128)} %bitcast.5, ...), kind=kOutput, calls=%fused_computation.62 | convolution fusion | flops 2178940928 | bytes 4194352 | tf_op jit(solution)/shard_map/dot_general | solution.py:91
  174.5 11.3 %all-to-all-start.1 = ((bf16[16,64,1024]{2,1,0:T(8,128)(2,1)}), bf16[16,64,1024]{2,1,0:T(8,128)(2,1)}, u32[]{:S(2)}, u32[]{:S(2)}) async-start(bf16[16,64,1024]{2,1,0:T(8,128)(2,1)} %fusion.123), calls=%async_computation.1 | async-start | bytes 4194304 | tf_op jit(solution)/shard_map/all_to_all | solution.py:29
  187.0 39.9 %all-to-all-done.1 = bf16[16,64,1024]{2,1,0:T(8,128)(2,1)} async-done(((bf16[16,64,1024]{2,1,0:T(8,128)(2,1)}), bf16[16,64,1024]{2,1,0:T(8,128)(2,1)}, u32[]{:S(2)}, u32[]{:S(2)}) %all-to-all-start.1) | async-done | bytes 2097184 | tf_op jit(solution)/shard_map/all_to_all | solution.py:29
  226.9 2.0 convert_bitcast_fusion
  229.0 4.4 copy.20
  233.4 5.0 reshape.104
  238.4 6.9 %multiply_reduce_fusion.1 = f32[]{:T(128)} fusion(f32[64,32,512]{2,1,0:T(8,128)} %param.17, f32[64,32,512]{2,1,0:T(8,128)} %reshape.104, f32[]{:T(128)} %bitcast.302, s32[64,32,512]{2,1,0:T(8,128)} %param.19, s32[64,512]{1,0:T(8,128)S(1)} %copy-done.1), kind=kLoop, calls=%fused_computation.31 | loop fusion | flops 7340031 | bytes 12713992 | tf_op jit(solution)/shard_map/reduce_sum | solution.py:94
  245.2 39.8 %psum.14 = f32[]{:T(128)} all-reduce(f32[]{:T(128)} %multiply_reduce_fusion.1), channel_id=1, replica_groups=mesh['parts'=2,'lon'=16] {'lon'}, use_global_device_ids=true, to_apply=%region_1.0 | all-reduce | flops 1 | bytes 8 | tf_op jit(solution)/shard_map/psum | solution.py:94
  285.8 10.5 %multiply_subtract_fusion = f32[64,32,512]{2,1,0:T(8,128)} fusion(f32[64,32,512]{2,1,0:T(8,128)} %param.16, f32[]{:T(128)S(6)} %div.110, f32[64,32,512]{2,1,0:T(8,128)} %reshape.104, f32[64,32,512]{2,1,0:T(8,128)} %param.17, f32[]{:T(128)} %bitcast.304, s32[64,32,512]{2,1,0:T(8,128)} %param.19, s32[64,512]{1,0:T(8,128)S(1)} %copy-done.1), kind=kLoop, calls=%fused_computation.29 | loop fusion | flops 7340032 | bytes 21102600 | tf_op jit(solution)/shard_map/sub | solution.py:97
  296.3 7.3 %fusion.54 = bf16[64,32,512]{2,1,0:T(8,128)(2,1)} fusion(f32[64,32,512]{2,1,0:T(8,128)} %multiply_subtract_fusion, s32[64,32,512]{2,1,0:T(8,128)} %param.19, s32[64,512]{1,0:T(8,128)S(1)} %copy-done.1, bf16[512,512]{1,0:T(8,128)(2,1)S(1)} %copy-done.2, bf16[32,32]{1,0:T(8,128)(2,1)S(1)} %copy-done.3), kind=kOutput, calls=%fused_computation.64 | convolution fusion | flops 1147142144 | bytes 11143168 | tf_op jit(solution)/shard_map/acj,jb->acb/dot_general | solution.py:48
  303.6 4.1 all_to_all.54
  307.6 2.7 copy.21
  310.4 50.1 %all_to_all.69 = bf16[64,16,1024]{2,0,1:T(8,128)(2,1)S(1)} all-to-all(bf16[64,16,1024]{2,0,1:T(8,128)(2,1)S(1)} %copy.21), channel_id=1, replica_groups=mesh['parts'=2,'lon'=16] {'lon'}, dimensions={1} | all-to-all | bytes 4194304 | tf_op jit(solution)/shard_map/all_to_all | solution.py:24
  360.5 2.4 convert_bitcast_fusion.2
  373.5 5.1 all-to-all-start.3
  379.5 2.4 mul.543
  381.8 5.2 mul.544
  387.1 32.7 %all-to-all-done.3 = bf16[16,64,1024]{2,1,0:T(8,128)(2,1)} async-done(((bf16[16,64,1024]{2,1,0:T(8,128)(2,1)}), bf16[16,64,1024]{2,1,0:T(8,128)(2,1)}, u32[]{:S(2)}, u32[]{:S(2)}) %all-to-all-start.3) | async-done | bytes 2097184 | tf_op jit(solution)/shard_map/all_to_all | solution.py:29
  419.8 5.3 fusion.16
  425.1 58.3 %all_to_all.70 = bf16[64,16,1024]{2,0,1:T(8,128)(2,1)S(1)} all-to-all(bf16[64,16,1024]{2,0,1:T(8,128)(2,1)S(1)} %fusion.16), channel_id=1, replica_groups=mesh['parts'=2,'lon'=16] {'lon'}, dimensions={1} | all-to-all | bytes 4194304 | tf_op jit(solution)/shard_map/all_to_all | solution.py:24
  483.4 2.4 convert_bitcast_fusion.1
  486.1 52.5 %all_to_all.71 = bf16[16,64,1024]{2,1,0:T(8,128)(2,1)S(1)} all-to-all(bf16[16,64,1024]{2,1,0:T(8,128)(2,1)S(1)} %fusion.91), channel_id=1, replica_groups=mesh['parts'=2,'lon'=16] {'lon'}, dimensions={0} | all-to-all | bytes 4194304 | tf_op jit(solution)/shard_map/all_to_all | solution.py:29
  538.6 2.5 copy.23
  541.1 4.1 reshape_reshape.2
  545.1 9.0 %multiply_reduce_fusion = (f32[]{:T(128)}, f32[64,32,512]{2,1,0:T(8,128)}) fusion(f32[64,32,512]{2,1,0:T(8,128)} %multiply_subtract_fusion, bf16[64,32,512]{2,1,0:T(8,128)(2,1)} %reshape_reshape.2, bf16[512,512]{1,0:T(8,128)(2,1)S(1)} %copy-done.2, bf16[32,32]{1,0:T(8,128)(2,1)S(1)} %copy-done.3, s32[64,32,512]{2,1,0:T(8,128)} %param.19, ...), kind=kOutput, calls=%fused_computation.27 | convolution fusion | flops 1147142144 | bytes 15337476 | tf_op jit(solution)/shard_map/ck,akb->acb/dot_general | solution.py:36
  554.1 33.7 %psum.15 = f32[]{:T(128)} all-reduce(f32[]{:T(128)} %get-tuple-element.45), channel_id=1, replica_groups=mesh['parts'=2,'lon'=16] {'lon'}, use_global_device_ids=true, to_apply=%region_3.0 | all-reduce | flops 1 | bytes 8 | tf_op jit(solution)/shard_map/psum | solution.py:112
  588.5 10.6 %multiply_add_fusion = (f32[64,32,512]{2,1,0:T(8,128)}, f32[64,32,512]{2,1,0:T(8,128)}) fusion(f32[64,32,512]{2,1,0:T(8,128)} %get-tuple-element.46, f32[64,32,512]{2,1,0:T(8,128)} %param.17, f32[]{:T(128)S(6)} %div.113, f32[64,32,512]{2,1,0:T(8,128)} %param.15, f32[]{:T(128)S(6)} %div.110), kind=kLoop, calls=%fused_computation.26 | loop fusion | flops 4194304 | bytes 20971528 | tf_op jit(solution)/shard_map/add | solution.py:114
  (69 shorter events, 25.8 us)
Async XLA Ops:
  0.6 359.9 %copy-start = (bf16[1024,1024]{1,0:T(8,128)(2,1)S(1)}, bf16[1024,1024]{1,0:T(8,128)(2,1)}, u32[]{:S(2)}) copy-start(bf16[1024,1024]{1,0:T(8,128)(2,1)} %param.22) | copy-start | bytes 6291460
  48.2 48.6 %all-to-all-start = ((bf16[64,16,1024]{2,0,1:T(8,128)(2,1)}), bf16[64,16,1024]{2,0,1:T(8,128)(2,1)}, u32[]{:S(2)}, u32[]{:S(2)}) async-start(bf16[64,16,1024]{2,0,1:T(8,128)(2,1)} %copy.19), calls=%async_computation | async-start | bytes 4194304 | tf_op jit(solution)/shard_map/all_to_all | solution.py:24
  174.5 52.4 %all-to-all-start.1 = ((bf16[16,64,1024]{2,1,0:T(8,128)(2,1)}), bf16[16,64,1024]{2,1,0:T(8,128)(2,1)}, u32[]{:S(2)}, u32[]{:S(2)}) async-start(bf16[16,64,1024]{2,1,0:T(8,128)(2,1)} %fusion.123), calls=%async_computation.1 | async-start | bytes 4194304 | tf_op jit(solution)/shard_map/all_to_all | solution.py:29
  233.4 5.0 copy-start.1
  285.7 10.6 %copy-start.2 = (bf16[512,512]{1,0:T(8,128)(2,1)S(1)}, bf16[512,512]{1,0:T(8,128)(2,1)}, u32[]{:S(2)}) copy-start(bf16[512,512]{1,0:T(8,128)(2,1)} %param.23) | copy-start | bytes 1572868
  285.8 10.5 %copy-start.3 = (bf16[32,32]{1,0:T(8,128)(2,1)S(1)}, bf16[32,32]{1,0:T(8,128)(2,1)}, u32[]{:S(2)}) copy-start(bf16[32,32]{1,0:T(8,128)(2,1)} %param.24) | copy-start | bytes 6148
  373.5 5.1 copy-start.4
  373.5 5.9 copy-start.5
  373.5 46.3 %all-to-all-start.3 = ((bf16[16,64,1024]{2,1,0:T(8,128)(2,1)}), bf16[16,64,1024]{2,1,0:T(8,128)(2,1)}, u32[]{:S(2)}, u32[]{:S(2)}) async-start(bf16[16,64,1024]{2,1,0:T(8,128)(2,1)} %fusion.107), calls=%async_computation.3 | async-start | bytes 4194304 | tf_op jit(solution)/shard_map/all_to_all | solution.py:29
